TPU v7x, 256 devices: a whole 4x4x8 slice. The times are simulated.
256 devices in a mesh: row: 8 (over z), col: 32 (over y, x, core).
Axes of the slice: x: 4, y: 4, z: 8, core: 2. Of those that a mesh axis runs over, the one named last changes fastest.
Arguments:
- tokens: bfloat16 [1024, 16384], P('col', 'row'), may hold values from -6 to 6
- gate_weight: bfloat16 [16384, 28672], P('row', 'col'), may hold values from -0.0625 to 0.0625
- up_weight: bfloat16 [16384, 28672], P('row', 'col'), may hold values from -0.0625 to 0.0625
- down_weight: bfloat16 [28672, 16384], P('col', 'row'), may hold values from -0.046875 to 0.046875
- gate_mask: int32 [128, 224], P('row', 'col'), may hold values 0 or 1
- up_mask: int32 [128, 224], P('row', 'col'), may hold values 0 or 1
- down_mask: int32 [224, 128], P('col', 'row'), may hold values 0 or 1
Outputs:
- ffn_out: bfloat16 [1024, 16384], P('col', 'row')
Inputs may be any that keep to these rules, and one draw needn't show every extreme that they name: `gate_mask`: 0 drops a block, 1 keeps it. `up_mask`: 0 drops a block, 1 keeps it. `down_mask`: 0 drops a block, 1 keeps it.
All inputs are finite; a program needn't handle non-finite values.
Results may differ from a plain program's by a relative error of at most 0.0049.
Values may be sent and summed in bfloat16 or wider, within the bound.
A program may use at most 128 MiB of HBM per device.

v0:
```python
import jax
import jax.numpy as jnp
from jax import lax
from jax.sharding import PartitionSpec as P

BLOCK = 128


def keep_blocks(weight, mask):
    rows, cols = mask.shape
    full = jnp.broadcast_to(mask[:, None, :, None], (rows, BLOCK, cols, BLOCK)).reshape(
        rows * BLOCK, cols * BLOCK
    )
    return weight * full.astype(weight.dtype)


def body(tokens, gate_weight, up_weight, down_weight, gate_mask, up_mask, down_mask):
    half = gate_weight.shape[1]
    paired = jnp.concatenate(
        [keep_blocks(gate_weight, gate_mask), keep_blocks(up_weight, up_mask)], axis=1
    )
    partial_terms = jnp.dot(
        lax.all_gather(tokens, "col", axis=0, tiled=True),
        paired,
        preferred_element_type=jnp.float32,
    )
    summed = lax.psum(partial_terms, "row")
    hidden = (jax.nn.silu(summed[:, :half]) * summed[:, half:]).astype(jnp.bfloat16)
    down_kept = keep_blocks(down_weight, down_mask)
    result = lax.psum_scatter(
        jnp.dot(hidden, down_kept, preferred_element_type=jnp.float32),
        "col",
        scatter_dimension=0,
        tiled=True,
    )
    return result.astype(jnp.bfloat16)


def solution(mesh):
    placed = (
        P("col", "row"),
        P("row", "col"),
        P("row", "col"),
        P("col", "row"),
        P("row", "col"),
        P("row", "col"),
        P("col", "row"),
    )
    return jax.shard_map(
        body, mesh=mesh, in_specs=placed, out_specs=P("col", "row"), check_vma=False
    )
```

profile of v0, /device:TPU:2, one launch (start us, length us, event | category | flops | bytes accessed | tf_op | source)
XLA Modules:
  0.0 365.8 jit_solution(14413557150695035963)
XLA Ops:
  6.5 0.0 all-gather.2.cloned.1.call-start
  6.5 0.7 all-gather.2.cloned.1.call-update
  7.3 0.0 all-reduce.2.cloned.1.call-start
  7.3 0.7 convert_element_type.27
  8.0 0.7 convert_element_type.29
  8.7 6.1 %copy.10 = bf16[2048,896]{0,1:T(8,128)(2,1)} copy(bf16[2048,896]{1,0:T(8,128)(2,1)} %param.8) | data formatting | bytes 7340032 | tf_op args[1]
  14.8 6.2 %copy.11 = bf16[2048,896]{0,1:T(8,128)(2,1)} copy(bf16[2048,896]{1,0:T(8,128)(2,1)} %param.9) | data formatting | bytes 7340032 | tf_op args[2]
  21.0 0.0 copy-start
  21.0 0.0 copy-start.1
  21.0 0.5 broadcast_in_dim.6
  21.5 0.5 broadcast_in_dim.7
  22.1 0.9 copy-done
  23.0 1.1 copy-done.1
  24.1 3.9 %bitcast_multiply_fusion.2 = (bf16[2048,896]{0,1:T(8,128)(2,1)}, bf16[2048,896]{0,1:T(8,128)(2,1)}) fusion(bf16[2048,896]{0,1:T(8,128)(2,1)S(1)} %copy-done.1, bf16[112,8,16,128]{3,2,1,0:T(8,128)(2,1)S(1)} %bitcast.21, bf16[2048,896]{0,1:T(8,128)(2,1)S(1)} %copy-done, bf16[112,8,16,128]{3,2,1,0:T(8,128)(2,1)S(1)} %bitcast.20), kind=kLoop, calls=%fused_computation.8 | loop fusion | flops 3670016 | bytes 22020096 | tf_op jit(solution)/shard_map/mul | solution.py:14
  28.0 35.7 %all-gather.2.cloned.1.call-done = bf16[1024,2048]{1,0:T(8,128)(2,1)} async-done(((bf16[32,2048]{1,0:T(8,128)(2,1)}), bf16[1024,2048]{1,0:T(8,128)(2,1)}) %all-gather.2.cloned.1.call-update) | async-done | bytes 4194320 | tf_op jit(solution)/shard_map/all_gather | solution.py:23
  63.7 13.7 %fusion.4 = f32[1024,1792]{0,1:T(8,128)} fusion(bf16[1024,2048]{1,0:T(8,128)(2,1)} %all-gather.2.cloned.1.call-done, bf16[2048,896]{0,1:T(8,128)(2,1)} %get-tuple-element.5, bf16[2048,896]{0,1:T(8,128)(2,1)} %get-tuple-element.6), kind=kOutput, calls=%fused_computation.4 | convolution fusion | flops 7530872832 | bytes 18874368 | tf_op jit(solution)/shard_map/dot_general | solution.py:22
  77.4 0.0 copy-start.2
  77.4 0.0 all-reduce.2.cloned.1.call-update
  77.4 0.0 reduce-scatter.2.cloned.1.call-start
  77.5 0.6 copy-done.2
  78.1 167.5 %all-reduce.2.cloned.1.call-done = f32[1024,1792]{0,1:T(8,128)} async-done(((f32[1024,1792]{0,1:T(8,128)}), f32[1024,1792]{0,1:T(8,128)}) %all-reduce.2.cloned.1.call-update) | async-done | bytes 7340048 | tf_op jit(solution)/shard_map/psum | solution.py:27
  245.6 0.0 copy-start.3
  245.6 0.5 broadcast_in_dim.8
  246.1 1.5 copy-done.3
  247.6 11.1 %fusion.7 = f32[1024,2048]{1,0:T(8,128)} fusion(bf16[896,2048]{1,0:T(8,128)(2,1)S(1)} %copy-done.3, bf16[112,8,16,128]{3,2,1,0:T(8,128)(2,1)S(1)} %bitcast.22, f32[1024,1792]{0,1:T(8,128)} %all-reduce.2.cloned.1.call-done), kind=kOutput, calls=%fused_computation.6 | convolution fusion | flops 3765436416 | bytes 23068672 | tf_op jit(solution)/shard_map/dot_general | solution.py:31
  258.7 0.0 reduce-scatter.2.cloned.1.call-update
  258.8 98.9 %reduce-scatter.2.cloned.1.call-done = f32[32,2048]{1,0:T(8,128)} async-done(((f32[1024,2048]{1,0:T(8,128)}), f32[32,2048]{1,0:T(8,128)}) %reduce-scatter.2.cloned.1.call-update) | async-done | bytes 262160 | tf_op jit(solution)/shard_map/reduce_scatter | solution.py:30
  357.6 1.6 convert_element_type.34
  (1 shorter events, 0.0 us)
Async XLA Ops:
  6.5 57.2 %all-gather.2.cloned.1.call-start = ((), (), s32[]{:S(2)}) async-start(), calls=%async_computation.1 | async-start | bytes 4325376 | tf_op jit(solution)/shard_map/all_gather | solution.py:23
  7.3 238.3 %all-reduce.2.cloned.1.call-start = ((), (), s32[]{:S(2)}) async-start(), calls=%async_computation.2 | async-start | bytes 14680064 | tf_op jit(solution)/shard_map/psum | solution.py:27
  21.0 2.0 copy-start
  21.0 3.2 copy-start.1
  77.4 0.7 copy-start.2
  77.4 280.2 %reduce-scatter.2.cloned.1.call-start = ((), (), s32[]{:S(2)}) async-start(), calls=%async_computation.3 | async-start | bytes 8650752 | tf_op jit(solution)/shard_map/reduce_scatter | solution.py:30
  245.6 2.0 copy-start.3
Sparse Core Ops, SparseCore 0:
  9.9 53.7 all-gather.1
  77.5 167.9 all-reduce.1
  258.9 98.7 reduce-scatter.1
where the time goes:
time: 366 us
  waiting for transfers between devices  303 us (83%)
  matrix products  24.8 us (7%)
  local copies, waits for them, and re-layouts  18.1 us (5%)
  between operations  13.1 us (4%)
  other arithmetic  6.87 us (2%)
    psum x1, waiting for transfers between devices, body(): summed = lax.psum(partial_terms, 'row')  167 us
    reduce_scatter x1, waiting for transfers between devices, body(): lax.psum_scatter(jnp.dot(hidden, down_kept, preferred_element_type=jnp.fl...  98.9 us
    all_gather x1, waiting for transfers between devices, body(): lax.all_gather(tokens, 'col', axis=0, tiled=True)  35.7 us
    unnamed x10, local copies, waits for them, and re-layouts  16.4 us
    dot_general x1, matrix products, body(): jnp.dot(lax.all_gather(tokens, 'col', axis=0, tiled=True), paired, prefer...  13.7 us
    dot_general x1, matrix products, body(): jnp.dot(hidden, down_kept, preferred_element_type=jnp.float32)  11.1 us
  transfers between devices with their start and end apart: 3, of which 3 were waited for; matrix products, arithmetic and copies ran while one was open for 5% of the time, Pallas kernels for 0%

commit v1 on v0

v1 whole, which is shorter than its diff:
```python
import functools

import jax
import jax.numpy as jnp
from jax import lax
from jax.experimental import pallas as pl
from jax.experimental.pallas import tpu as pltpu
from jax.sharding import PartitionSpec as P

MESH = pl.DeviceIdType.MESH
BLOCK = 128
ROWS = 8
SIDE = 4
CORES = 2
CHUNKS = 8
OWN = 16
WIDTH = 256
BF16 = jnp.bfloat16
F32 = jnp.float32


def kernel(
    gate_mask, up_mask, down_mask, tokens, gate_weight, up_weight, down_weight, out,
    pair, down, tok, part, msg_out, msg_in, low_out, low_in, wide_out, wide_in,
    hid, term, sibling, out_send, out_recv,
    w_sem, tok_own, tok_send, tok_recv, fwd_send, fwd_recv,
    msg_send, msg_recv, low_send, low_recv, wide_send, wide_recv,
    ag_send, ag_recv, ex_send, ex_recv, res_send, res_recv,
):
    z = lax.axis_index("row")
    col = lax.axis_index("col")
    core = lax.rem(col, CORES)
    chip = lax.div(col, CORES)
    x = lax.rem(chip, SIDE)
    y = lax.div(chip, SIDE)
    ff = gate_weight.shape[1]
    depth = gate_weight.shape[0]
    halves = (slice(0, ff), slice(ff, 2 * ff))

    def ring(step):
        return lax.rem(z + step + ROWS, ROWS)

    def at_offset(j, sign, to_core):
        dx, dy = lax.rem(j, SIDE), lax.div(j, SIDE)
        x2 = lax.rem(x + sign * dx + SIDE, SIDE)
        y2 = lax.rem(y + sign * dy + SIDE, SIDE)
        return (z, (y2 * SIDE + x2) * CORES + to_core)

    def remote(src, dst, send, recv, device):
        return pltpu.make_async_remote_copy(
            src_ref=src, dst_ref=dst, send_sem=send, recv_sem=recv,
            device_id=device, device_id_type=MESH,
        )

    mate = (z, chip * CORES + 1 - core)
    neighbour = ((ring(1), col), (ring(-1), col))

    quarter = depth // 4
    w_copies = []
    for i in range(4):
        rows = slice(i * quarter, (i + 1) * quarter)
        for h, w in enumerate((gate_weight, up_weight)):
            w_copies.append(
                pltpu.make_async_copy(w.at[rows], pair.at[rows, halves[h]], w_sem.at[h, i])
            )
    d_copy = pltpu.make_async_copy(down_weight, down, w_sem.at[2, 0])
    own_copy = pltpu.make_async_copy(tokens, tok.at[0, 0, core], tok_own)
    own_copy.start()
    for copy in w_copies:
        copy.start()
    d_copy.start()

    barrier = pltpu.get_barrier_semaphore()
    pl.semaphore_signal(barrier, inc=1, device_id=mate, device_id_type=MESH)
    for side in range(2):
        pl.semaphore_signal(barrier, inc=1, device_id=neighbour[side], device_id_type=MESH)

    @pl.loop(1, SIDE * SIDE)
    def _(j):
        pl.semaphore_signal(barrier, inc=1, device_id=at_offset(j, 1, core), device_id_type=MESH)

    pl.semaphore_wait(barrier, SIDE * SIDE - 1 + 3)

    def tok_copy(j):
        k, p = lax.div(j, 2), lax.rem(j, 2)
        return remote(
            tokens, tok.at[k, p, core], tok_send.at[j], tok_recv.at[j], at_offset(j, -1, core)
        )

    def fwd_copy(k):
        return remote(tok.at[k, :, core], tok.at[k, :, core], fwd_send.at[k], fwd_recv.at[k], mate)

    def msg_copy(side, s, c):
        src, dst = msg_out.at[side, s, c], msg_in.at[side, s, c]
        if s == 0:
            src, dst = src.at[:, halves[side]], dst.at[:, halves[side]]
        return remote(src, dst, msg_send.at[side, s, c], msg_recv.at[side, s, c], neighbour[side])

    def low_copy(side, c):
        return remote(
            low_out.at[side, c], low_in.at[side, c],
            low_send.at[side, c], low_recv.at[side, c], neighbour[side],
        )

    def wide_copy(side, c):
        return remote(
            wide_out.at[side, c], wide_in.at[side, c],
            wide_send.at[side, c], wide_recv.at[side, c], neighbour[side],
        )

    cut = 4 * BLOCK

    def ag_ref(side, s, c, owner):
        ref = hid.at[c, owner]
        if s == 3:
            ref = ref.at[:, slice(0, cut) if side == 0 else slice(cut, ff)]
        return ref

    def ag_copy(side, s, c):
        block = ag_ref(side, s, c, ring(-s if side == 0 else s))
        return remote(block, block, ag_send.at[side, s, c], ag_recv.at[side, s, c], neighbour[side])

    def ex_copy(c):
        return remote(
            term.at[c, :, 1 - core], sibling.at[c], ex_send.at[c], ex_recv.at[c], mate
        )

    def res_copy(j):
        k, p = lax.div(j, 2), lax.rem(j, 2)
        return remote(
            out_send.at[k, p], out_recv.at[j], res_send.at[j], res_recv.at[j], at_offset(j, 1, core)
        )

    def keep(ref, rows, lanes, flag):
        scale = jnp.full((BLOCK, BLOCK), flag.astype(F32), F32).astype(BF16)
        ref[rows, lanes] = ref[rows, lanes] * scale

    def mask_pair(i):
        @pl.loop(0, quarter // BLOCK)
        def _(r):
            block = i * (quarter // BLOCK) + r
            rows = pl.ds(pl.multiple_of(block * BLOCK, BLOCK), BLOCK)
            for h, mask in enumerate((gate_mask, up_mask)):
                for b in range(ff // BLOCK):
                    start = h * ff + b * BLOCK
                    keep(pair, rows, slice(start, start + BLOCK), mask[block, b])

    def mask_down():
        @pl.loop(0, ff // BLOCK)
        def _(r):
            rows = pl.ds(pl.multiple_of(r * BLOCK, BLOCK), BLOCK)
            for b in range(down.shape[1] // BLOCK):
                keep(down, rows, slice(b * BLOCK, (b + 1) * BLOCK), down_mask[r, b])

    def first_matmul(c):
        @pl.loop(0, 2 * ff // WIDTH)
        def _(n):
            lanes = pl.ds(pl.multiple_of(n * WIDTH, WIDTH), WIDTH)
            value = jnp.dot(
                tok[c].reshape(CHUNKS * OWN, depth), pair[:, lanes], preferred_element_type=F32
            )
            part[c, :, :, lanes] = value.reshape(ROWS, OWN, WIDTH)

    def down_matmul(c):
        @pl.loop(0, down.shape[1] // WIDTH)
        def _(n):
            lanes = pl.ds(pl.multiple_of(n * WIDTH, WIDTH), WIDTH)
            value = jnp.dot(
                hid[c].reshape(ROWS * OWN, ff), down[:, lanes], preferred_element_type=F32
            )
            term[c, :, :, :, lanes] = value.reshape(2, CORES, 2 * OWN, WIDTH)

    def sum_start(c):
        owner = ring(4)
        for side in range(2):
            h = halves[side]
            msg_out[side, 0, c, :, h] = part[c, owner, :, h].astype(BF16)
            msg_copy(side, 0, c).start()

    def sum_step(s, c):
        for side in range(2):
            owner = ring(4 - s if side == 0 else s - 4)
            msg_copy(side, s - 1, c).wait_recv()
            for h in range(2):
                lanes = halves[h]
                value = part[c, owner, :, lanes]
                if s > 1 or h == side:
                    value = value + msg_in[side, s - 1, c, :, lanes].astype(F32)
                if s < 3:
                    msg_out[side, s, c, :, lanes] = value.astype(BF16)
                elif h == side:
                    wide_out[side, c] = value
                else:
                    low_out[side, c] = value.astype(BF16)
            if s < 3:
                msg_copy(side, s, c).start()
            else:
                wide_copy(side, c).start()
                low_copy(side, c).start()

    def sum_end(c):
        for side in range(2):
            wide_copy(side, c).wait_recv()
            low_copy(side, c).wait_recv()
        gate = part[c, z, :, halves[0]] + wide_in[0, c] + low_in[1, c].astype(F32)
        up = part[c, z, :, halves[1]] + wide_in[1, c] + low_in[0, c].astype(F32)
        hid[c, z] = (gate / (1.0 + jnp.exp(-gate)) * up).astype(BF16)
        for side in range(2):
            ag_copy(side, 0, c).start()

    def gather_step(s, c):
        for side in range(2):
            ag_copy(side, s - 1, c).wait_recv()
            ag_copy(side, s, c).start()

    def gather_end(c):
        for side in range(2):
            ag_copy(side, 3, c).wait_recv()
        down_matmul(c)
        ex_copy(c).start()

    def send_result(c):
        ex_copy(c).wait_recv()
        for p in range(2):
            value = term[c, p, core] + sibling[c, p]
            term[c, p, core] = value
            out_send[c, p] = value.astype(BF16)
            if p == 1:
                res_copy(2 * c + p).start()
            else:
                @pl.when(c > 0)
                def _():
                    res_copy(2 * c).start()

    tok_copy(1).start()
    for j in (2, 3):
        tok_copy(j).start()
    for i in range(4):
        w_copies[2 * i].wait()
        w_copies[2 * i + 1].wait()
        mask_pair(i)
    own_copy.wait()
    tok_copy(1).wait_recv()
    fwd_copy(0).start()

    def at(c, stage, *args):
        @pl.when(jnp.logical_and(c >= 0, c < CHUNKS))
        def _():
            stage(*args, c)

    @pl.loop(0, CHUNKS + 9)
    def _(t):
        @pl.when(t + 2 < CHUNKS)
        def _():
            tok_copy(2 * t + 4).start()
            tok_copy(2 * t + 5).start()

        for s in (3, 2, 1):
            at(t - 4 - s, gather_step, s)
        at(t - 4, sum_end)
        for s in (3, 2, 1):
            at(t - s, sum_step, s)

        @pl.when(t + 1 < CHUNKS)
        def _():
            tok_copy(2 * t + 2).wait_recv()
            tok_copy(2 * t + 3).wait_recv()
            fwd_copy(t + 1).start()

        @pl.when(t < CHUNKS)
        def _():
            fwd_copy(t).wait_recv()
            first_matmul(t)
            sum_start(t)

        @pl.when(t == 1)
        def _():
            d_copy.wait()
            mask_down()

        at(t - 9, send_result)
        at(t - 8, gather_end)


    def add(j, _):
        res_copy(j).wait_recv()
        term[0, 0, core] = term[0, 0, core] + out_recv[j].astype(F32)
        return 0

    lax.fori_loop(1, SIDE * SIDE, add, 0)
    out[...] = term[0, 0, core].astype(BF16)

    @pl.loop(0, CHUNKS)
    def _(c):
        for side in range(2):
            for s in range(3):
                msg_copy(side, s, c).wait_send()
            low_copy(side, c).wait_send()
            wide_copy(side, c).wait_send()
            for s in range(4):
                ag_copy(side, s, c).wait_send()
        fwd_copy(c).wait_send()
        ex_copy(c).wait_send()

    @pl.loop(1, SIDE * SIDE)
    def _(j):
        tok_copy(j).wait_send()
        res_copy(j).wait_send()


def body(tokens, gate_weight, up_weight, down_weight, gate_mask, up_mask, down_mask):
    depth, ff = gate_weight.shape
    wide = down_weight.shape[1]
    own_tokens = tokens.shape[0]
    dma = pltpu.SemaphoreType.DMA
    chips = SIDE * SIDE
    smem = pl.BlockSpec(memory_space=pltpu.SMEM)
    anywhere = pl.BlockSpec(memory_space=pl.ANY)
    n_tokens = own_tokens * chips * CORES
    return pl.pallas_call(
        kernel,
        out_shape=jax.ShapeDtypeStruct((own_tokens, wide), BF16),
        in_specs=[smem] * 3 + [anywhere] * 4,
        out_specs=pl.BlockSpec(memory_space=pltpu.VMEM),
        scratch_shapes=[
            pltpu.VMEM((depth, 2 * ff), BF16),
            pltpu.VMEM((ff, wide), BF16),
            pltpu.VMEM((CHUNKS, 2, CORES, own_tokens, depth), BF16),
            pltpu.VMEM((CHUNKS, ROWS, OWN, 2 * ff), F32),
            pltpu.VMEM((2, 3, CHUNKS, OWN, 2 * ff), BF16),
            pltpu.VMEM((2, 3, CHUNKS, OWN, 2 * ff), BF16),
            pltpu.VMEM((2, CHUNKS, OWN, ff), BF16),
            pltpu.VMEM((2, CHUNKS, OWN, ff), BF16),
            pltpu.VMEM((2, CHUNKS, OWN, ff), F32),
            pltpu.VMEM((2, CHUNKS, OWN, ff), F32),
            pltpu.VMEM((CHUNKS, ROWS, OWN, ff), BF16),
            pltpu.VMEM((CHUNKS, 2, CORES, own_tokens, wide), F32),
            pltpu.VMEM((CHUNKS, 2, own_tokens, wide), F32),
            pltpu.VMEM((CHUNKS, 2, own_tokens, wide), BF16),
            pltpu.VMEM((chips, own_tokens, wide), BF16),
            dma((3, 4)),
            dma,
            dma((chips,)), dma((chips,)),
            dma((CHUNKS,)), dma((CHUNKS,)),
            dma((2, 3, CHUNKS)), dma((2, 3, CHUNKS)),
            dma((2, CHUNKS)), dma((2, CHUNKS)),
            dma((2, CHUNKS)), dma((2, CHUNKS)),
            dma((2, 4, CHUNKS)), dma((2, 4, CHUNKS)),
            dma((CHUNKS,)), dma((CHUNKS,)),
            dma((chips,)), dma((chips,)),
        ],
        compiler_params=pltpu.CompilerParams(
            collective_id=0, has_side_effects=True, vmem_limit_bytes=60 * 2**20
        ),
        cost_estimate=pl.CostEstimate(
            flops=6 * n_tokens * depth * ff,
            bytes_accessed=6 * depth * ff,
            transcendentals=n_tokens * ff // ROWS,
        ),
    )(gate_mask, up_mask, down_mask, tokens, gate_weight, up_weight, down_weight)


def solution(mesh):
    placed = (
        P("col", "row"),
        P("row", "col"),
        P("row", "col"),
        P("col", "row"),
        P("row", "col"),
        P("row", "col"),
        P("col", "row"),
    )
    return jax.shard_map(
        body, mesh=mesh, in_specs=placed, out_specs=P("col", "row"), check_vma=False
    )
```

time: 366 us -> 132 us (0.36)
  waiting for transfers between devices: 303 us -> 0 us
  Pallas kernels: 0 us -> 127 us
  matrix products: 24.8 us -> 0 us
  local copies, waits for them, and re-layouts: 18.1 us -> 4.28 us
  between operations: 13.1 us -> 0.01 us
  other arithmetic: 6.87 us -> 0 us
    psum x1 -> x0, waiting for transfers between devices: 167 us -> none  [body(): summed = lax.psum(partial_terms, 'row')]
    pallas_call x0 -> x1, Pallas kernels: none -> 127 us  [body(): pl.pallas_call(kernel, out_shape=jax.ShapeDtypeStruct((own_tokens, wide),...]
    reduce_scatter x1 -> x0, waiting for transfers between devices: 98.9 us -> none  [body(): lax.psum_scatter(jnp.dot(hidden, down_kept, preferred_element_type=jnp.fl...]
    all_gather x1 -> x0, waiting for transfers between devices: 35.7 us -> none  [body(): lax.all_gather(tokens, 'col', axis=0, tiled=True)]
    dot_general x2 -> x0, matrix products: 24.8 us -> none  [the longest x1 13.7 us: body(): jnp.dot(lax.all_gather(tokens, 'col', axis=0, tiled=True), paired, prefer...]
    unnamed x10 -> x3, local copies, waits for them, and re-layouts: 16.4 us -> 4.28 us
    mul x1 -> x0, other arithmetic: 3.87 us -> none  [keep_blocks(): return weight * full.astype(weight.dtype)]
  transfers between devices with their start and end apart: 3 -> 0, of which waited for: 3 -> 0; matrix products, arithmetic and copies ran while one was open for 5% -> 0% of each run, Pallas kernels for 0% -> 0%
where the time goes in v1:
time: 132 us; the launch traced here: 131 us
  Pallas kernels  127 us (96%)
  local copies, waits for them, and re-layouts  4.28 us (3%)
    pallas_call x1, Pallas kernels, body(): pl.pallas_call(kernel, out_shape=jax.ShapeDtypeStruct((own_tokens, wide),...  127 us
    unnamed x3, local copies, waits for them, and re-layouts  4.28 us

profile of v1, /device:TPU:2, one launch (start us, length us, event | category | flops | bytes accessed | tf_op | source)
XLA Modules:
  0.0 131.5 jit_solution(2151303013081617682)
XLA Ops:
  0.0 1.4 %copy.8.gate_mask = s32[16,7]{1,0:T(8,128)} copy(s32[16,7]{0,1:T(8,128)} %param.11) | data formatting | bytes 896 | tf_op args[4]
  1.4 1.4 %copy.9.up_mask = s32[16,7]{1,0:T(8,128)} copy(s32[16,7]{0,1:T(8,128)} %param.12) | data formatting | bytes 896 | tf_op args[5]
  2.7 127.2 %shard_map.73 = bf16[32,2048]{1,0:T(8,128)(2,1)} custom-call(s32[16,7]{1,0:T(8,128)} %copy.8.gate_mask, s32[16,7]{1,0:T(8,128)} %copy.9.up_mask, s32[7,16]{1,0:T(8,128)} %down_mask.1, bf16[32,2048]{1,0:T(8,128)(2,1)} %tokens.1, bf16[2048,896]{1,0:T(8,128)(2,1)} %gate_weight.1, bf16[2048,896]{1,0:T(8,128)(2,1)} %up_weight.1, bf16[896,2048]{1,0:T(8,128)(2,1)} %down_weight.1), custom_call_target="tpu_custom_call" | custom-call | flops 11274289152 | bytes 11010048 | tf_op jit(solution)/shard_map/pallas_call | solution.py:320
  129.9 1.6 %copy.11 = bf16[32,2048]{1,0:T(8,128)(2,1)} copy(bf16[32,2048]{1,0:T(8,128)(2,1)} %shard_map.73) | data formatting | bytes 262144

commit v2 on v1

--- a/solution.py
+++ b/solution.py
@@ -14,7 +14,72 @@
 CORES = 2
 CHUNKS = 8
 OWN = 16
-WIDTH = 256
+WIDTH1 = 896
+WIDTH2 = 1024
+GROUP = 1
+AHEAD = 2
+OFFSETS = (
+    ((0, 0), (1, 0)),
+    ((3, 0), (0, 1)),
+    ((1, 1), (0, 2)),
+    ((2, 1), (1, 2)),
+    ((3, 2), (2, 3)),
+    ((2, 2), (3, 3)),
+    ((3, 1), (1, 3)),
+    ((0, 3), (2, 0)),
+)
+OWN_PLACE = (0, 0)
+WAVES = (
+    (
+        (0, 1, (1, 0), OWN_PLACE),
+        (1, 0, (-1, 0), OWN_PLACE),
+        (1, 1, (0, 1), OWN_PLACE),
+        (7, 0, (0, -1), OWN_PLACE),
+    ),
+    (
+        (2, 0, (0, 1), (0, 1)),
+        (2, 1, (0, -1), (7, 0)),
+        (6, 1, (1, 0), (7, 0)),
+        (6, 0, (-1, 0), (1, 1)),
+    ),
+    (
+        (3, 0, (1, 0), (2, 0)),
+        (3, 1, (0, 1), (2, 0)),
+        (4, 0, (-1, 0), (2, 1)),
+        (4, 1, (1, 0), (6, 1)),
+    ),
+    (
+        (5, 0, (1, 0), (3, 1)),
+        (5, 1, (0, -1), (1, 0)),
+        (7, 1, (-1, 0), (1, 0)),
+    ),
+)
+DOUBLE = 1
+SLOTS = CHUNKS - DOUBLE
+ORDER = (
+    "bring_early",
+    "gather2",
+    "gather1",
+    "prepare_down",
+    "gather_end",
+    "sum_end",
+    "sum3",
+    "sum2",
+    "sum1",
+    "bring_late",
+    "matmul",
+    "send_result",
+    "collect",
+)
+DX, DY = (
+    tuple(sum(pair[p][i] * 4**k for k, pair in enumerate(OFFSETS)) for p in range(2))
+    for i in range(2)
+)
+
+
+def pick(digits, k):
+    return lax.rem(lax.shift_right_logical(jnp.int32(digits), jnp.int32(2 * k)), 4)
+
 BF16 = jnp.bfloat16
 F32 = jnp.float32
 
@@ -22,7 +87,7 @@
 def kernel(
     gate_mask, up_mask, down_mask, tokens, gate_weight, up_weight, down_weight, out,
     pair, down, tok, part, msg_out, msg_in, low_out, low_in, wide_out, wide_in,
-    hid, term, sibling, out_send, out_recv,
+    hid, term, sibling, out_send, out_recv, acc,
     w_sem, tok_own, tok_send, tok_recv, fwd_send, fwd_recv,
     msg_send, msg_recv, low_send, low_recv, wide_send, wide_recv,
     ag_send, ag_recv, ex_send, ex_recv, res_send, res_recv,
@@ -40,8 +105,8 @@
     def ring(step):
         return lax.rem(z + step + ROWS, ROWS)
 
-    def at_offset(j, sign, to_core):
-        dx, dy = lax.rem(j, SIDE), lax.div(j, SIDE)
+    def at_offset(k, p, sign, to_core):
+        dx, dy = pick(DX[p], k), pick(DY[p], k)
         x2 = lax.rem(x + sign * dx + SIDE, SIDE)
         y2 = lax.rem(y + sign * dy + SIDE, SIDE)
         return (z, (y2 * SIDE + x2) * CORES + to_core)
@@ -54,6 +119,7 @@
 
     mate = (z, chip * CORES + 1 - core)
     neighbour = ((ring(1), col), (ring(-1), col))
+    second = ((ring(2), col), (ring(-2), col))
 
     quarter = depth // 4
     w_copies = []
@@ -64,7 +130,7 @@
                 pltpu.make_async_copy(w.at[rows], pair.at[rows, halves[h]], w_sem.at[h, i])
             )
     d_copy = pltpu.make_async_copy(down_weight, down, w_sem.at[2, 0])
-    own_copy = pltpu.make_async_copy(tokens, tok.at[0, 0, core], tok_own)
+    own_copy = pltpu.make_async_copy(tokens, tok.at[OWN_PLACE[0], OWN_PLACE[1], core], tok_own)
     own_copy.start()
     for copy in w_copies:
         copy.start()
@@ -74,17 +140,35 @@
     pl.semaphore_signal(barrier, inc=1, device_id=mate, device_id_type=MESH)
     for side in range(2):
         pl.semaphore_signal(barrier, inc=1, device_id=neighbour[side], device_id_type=MESH)
-
-    @pl.loop(1, SIDE * SIDE)
-    def _(j):
-        pl.semaphore_signal(barrier, inc=1, device_id=at_offset(j, 1, core), device_id_type=MESH)
-
-    pl.semaphore_wait(barrier, SIDE * SIDE - 1 + 3)
-
-    def tok_copy(j):
-        k, p = lax.div(j, 2), lax.rem(j, 2)
+        pl.semaphore_signal(barrier, inc=1, device_id=second[side], device_id_type=MESH)
+
+    def others(k, p, run):
+        if p == 1:
+            run()
+        else:
+            pl.when(k > 0)(run)
+
+    @pl.loop(0, CHUNKS)
+    def _(k):
+        for p in range(2):
+            others(k, p, lambda: pl.semaphore_signal(
+                barrier, inc=1, device_id=at_offset(k, p, 1, core), device_id_type=MESH
+            ))
+
+    pl.semaphore_wait(barrier, SIDE * SIDE - 1 + 5)
+
+    def send_wave(number):
+        for k, p, (dx, dy), (from_k, from_p) in WAVES[number]:
+            x2, y2 = lax.rem(x - dx + SIDE, SIDE), lax.rem(y - dy + SIDE, SIDE)
+            src = tokens if number == 0 else tok.at[from_k, from_p, core]
+            remote(
+                src, tok.at[k, p, core], tok_send.at[k, p], tok_recv.at[k, p],
+                (z, (y2 * SIDE + x2) * CORES + core),
+            ).start()
+
+    def tok_wait(k, p):
         return remote(
-            tokens, tok.at[k, p, core], tok_send.at[j], tok_recv.at[j], at_offset(j, -1, core)
+            tok.at[k, p, core], tok.at[k, p, core], tok_send.at[k, p], tok_recv.at[k, p], mate
         )
 
     def fwd_copy(k):
@@ -117,18 +201,20 @@
         return ref
 
     def ag_copy(side, s, c):
-        block = ag_ref(side, s, c, ring(-s if side == 0 else s))
-        return remote(block, block, ag_send.at[side, s, c], ag_recv.at[side, s, c], neighbour[side])
+        far = min(s, 2)
+        block = ag_ref(side, s, c, ring(-far if side == 0 else far))
+        device = second[side] if s == 3 else neighbour[side]
+        return remote(block, block, ag_send.at[side, s, c], ag_recv.at[side, s, c], device)
 
     def ex_copy(c):
         return remote(
             term.at[c, :, 1 - core], sibling.at[c], ex_send.at[c], ex_recv.at[c], mate
         )
 
-    def res_copy(j):
-        k, p = lax.div(j, 2), lax.rem(j, 2)
+    def res_copy(k, p):
         return remote(
-            out_send.at[k, p], out_recv.at[j], res_send.at[j], res_recv.at[j], at_offset(j, 1, core)
+            out_send.at[k, p], out_recv.at[k, p], res_send.at[k, p], res_recv.at[k, p],
+            at_offset(k, p, 1, core),
         )
 
     def keep(ref, rows, lanes, flag):
@@ -145,30 +231,30 @@
                     start = h * ff + b * BLOCK
                     keep(pair, rows, slice(start, start + BLOCK), mask[block, b])
 
-    def mask_down():
-        @pl.loop(0, ff // BLOCK)
-        def _(r):
-            rows = pl.ds(pl.multiple_of(r * BLOCK, BLOCK), BLOCK)
-            for b in range(down.shape[1] // BLOCK):
-                keep(down, rows, slice(b * BLOCK, (b + 1) * BLOCK), down_mask[r, b])
+    def mask_down(r):
+        rows = pl.ds(pl.multiple_of(r * BLOCK, BLOCK), BLOCK)
+        for b in range(down.shape[1] // BLOCK):
+            keep(down, rows, slice(b * BLOCK, (b + 1) * BLOCK), down_mask[r, b])
 
     def first_matmul(c):
-        @pl.loop(0, 2 * ff // WIDTH)
+        @pl.loop(0, 2 * ff // WIDTH1)
         def _(n):
-            lanes = pl.ds(pl.multiple_of(n * WIDTH, WIDTH), WIDTH)
+            lanes = pl.ds(pl.multiple_of(n * WIDTH1, WIDTH1), WIDTH1)
             value = jnp.dot(
-                tok[c].reshape(CHUNKS * OWN, depth), pair[:, lanes], preferred_element_type=F32
+                tok[pl.ds(c, GROUP)].reshape(GROUP * ROWS * OWN, depth),
+                pair[:, lanes],
+                preferred_element_type=F32,
             )
-            part[c, :, :, lanes] = value.reshape(ROWS, OWN, WIDTH)
+            part[pl.ds(c, GROUP), :, :, lanes] = value.reshape(GROUP, ROWS, OWN, WIDTH1)
 
     def down_matmul(c):
-        @pl.loop(0, down.shape[1] // WIDTH)
+        @pl.loop(0, down.shape[1] // WIDTH2)
         def _(n):
-            lanes = pl.ds(pl.multiple_of(n * WIDTH, WIDTH), WIDTH)
+            lanes = pl.ds(pl.multiple_of(n * WIDTH2, WIDTH2), WIDTH2)
             value = jnp.dot(
                 hid[c].reshape(ROWS * OWN, ff), down[:, lanes], preferred_element_type=F32
             )
-            term[c, :, :, :, lanes] = value.reshape(2, CORES, 2 * OWN, WIDTH)
+            term[c, :, :, :, lanes] = value.reshape(2, CORES, 2 * OWN, WIDTH2)
 
     def sum_start(c):
         owner = ring(4)
@@ -212,9 +298,12 @@
         for side in range(2):
             ag_copy(side, s - 1, c).wait_recv()
             ag_copy(side, s, c).start()
+            if s == 2:
+                ag_copy(side, 3, c).start()
 
     def gather_end(c):
         for side in range(2):
+            ag_copy(side, 2, c).wait_recv()
             ag_copy(side, 3, c).wait_recv()
         down_matmul(c)
         ex_copy(c).start()
@@ -225,70 +314,108 @@
             value = term[c, p, core] + sibling[c, p]
             term[c, p, core] = value
             out_send[c, p] = value.astype(BF16)
-            if p == 1:
-                res_copy(2 * c + p).start()
-            else:
-                @pl.when(c > 0)
-                def _():
-                    res_copy(2 * c).start()
-
-    tok_copy(1).start()
-    for j in (2, 3):
-        tok_copy(j).start()
+            others(c, p, lambda: res_copy(c, p).start())
+
+    send_wave(0)
     for i in range(4):
         w_copies[2 * i].wait()
         w_copies[2 * i + 1].wait()
         mask_pair(i)
     own_copy.wait()
-    tok_copy(1).wait_recv()
-    fwd_copy(0).start()
-
-    def at(c, stage, *args):
-        @pl.when(jnp.logical_and(c >= 0, c < CHUNKS))
+    for k, p, _, _ in WAVES[0]:
+        tok_wait(k, p).wait_recv()
+    send_wave(1)
+    for k in range(2):
+        fwd_copy(k).start()
+
+    def at(slot, stage, *args):
+        @pl.when(jnp.logical_and(slot >= 0, slot < SLOTS))
         def _():
-            stage(*args, c)
-
-    @pl.loop(0, CHUNKS + 9)
-    def _(t):
-        @pl.when(t + 2 < CHUNKS)
-        def _():
-            tok_copy(2 * t + 4).start()
-            tok_copy(2 * t + 5).start()
-
-        for s in (3, 2, 1):
-            at(t - 4 - s, gather_step, s)
-        at(t - 4, sum_end)
-        for s in (3, 2, 1):
-            at(t - s, sum_step, s)
-
-        @pl.when(t + 1 < CHUNKS)
-        def _():
-            tok_copy(2 * t + 2).wait_recv()
-            tok_copy(2 * t + 3).wait_recv()
-            fwd_copy(t + 1).start()
-
-        @pl.when(t < CHUNKS)
-        def _():
-            fwd_copy(t).wait_recv()
-            first_matmul(t)
-            sum_start(t)
-
-        @pl.when(t == 1)
+            double = slot < DOUBLE
+            first = jnp.where(double, 2 * slot, slot + DOUBLE)
+
+            @pl.loop(first, first + jnp.where(double, 2, 1))
+            def _(c):
+                stage(*args, c)
+
+    def bring(t, plan):
+        for slot, places, chunks, wave in plan:
+            @pl.when(t == slot)
+            def _():
+                for place in places:
+                    tok_wait(*place).wait_recv()
+                for k in chunks:
+                    fwd_copy(k).start()
+                if wave is not None:
+                    send_wave(wave)
+
+    def bring_late(t):
+        bring(t, (
+            (1, ((2, 0), (2, 1), (6, 0), (6, 1)), (2,), 2),
+            (2, ((3, 0), (3, 1)), (3,), 3),
+        ))
+
+    def bring_early(t):
+        bring(t, (
+            (3, ((4, 0), (4, 1)), (4,), None),
+            (4, ((5, 0), (5, 1)), (5, 6), None),
+            (5, ((7, 1),), (7,), None),
+        ))
+
+    def matmul(c):
+        fwd_copy(c).wait_recv()
+        first_matmul(c)
+        sum_start(c)
+
+    def prepare_down(t):
+        @pl.when(t == 0)
         def _():
             d_copy.wait()
-            mask_down()
-
-        at(t - 9, send_result)
-        at(t - 8, gather_end)
-
-
-    def add(j, _):
-        res_copy(j).wait_recv()
-        term[0, 0, core] = term[0, 0, core] + out_recv[j].astype(F32)
-        return 0
-
-    lax.fori_loop(1, SIDE * SIDE, add, 0)
-    out[...] = term[0, 0, core].astype(BF16)
+
+        @pl.when(t < ff // BLOCK)
+        def _():
+            mask_down(t)
+
+    def collect(c):
+        for p in range(2):
+            others(c, p, lambda: res_copy(c, p).wait_recv())
+
+        @pl.when(c == 0)
+        def _():
+            acc[...] = term[0, 0, core] + out_recv[0, 1].astype(F32)
+
+        @pl.when(c > 0)
+        def _():
+            acc[...] = acc[...] + (out_recv[c, 0].astype(F32) + out_recv[c, 1].astype(F32))
+
+    stages = {
+        "bring_late": bring_late,
+        "bring_early": bring_early,
+        "prepare_down": prepare_down,
+        "matmul": lambda t: at(t, matmul),
+        "sum1": lambda t: at(t - 1, sum_step, 1),
+        "sum2": lambda t: at(t - 2, sum_step, 2),
+        "sum3": lambda t: at(t - 3, sum_step, 3),
+        "sum_end": lambda t: at(t - 4, sum_end),
+        "gather1": lambda t: at(t - 5, gather_step, 1),
+        "gather2": lambda t: at(t - 6, gather_step, 2),
+        "gather_end": lambda t: at(t - 7, gather_end),
+        "send_result": lambda t: at(t - 7, send_result),
+        "collect": lambda t: at(t - 9, collect),
+    }
+
+    @pl.loop(0, SLOTS + 7)
+    def _(t):
+        for name in ORDER:
+            stages[name](t)
+
+    late = ((6, 0), (6, 1), (7, 0), (7, 1))
+    for place in late:
+        res_copy(*place).wait_recv()
+    total = acc[...]
+    for k, p in late:
+        total = total + out_recv[k, p].astype(F32)
+    out[...] = total.astype(BF16)
 
     @pl.loop(0, CHUNKS)
     def _(c):
@@ -302,10 +429,11 @@
         fwd_copy(c).wait_send()
         ex_copy(c).wait_send()
 
-    @pl.loop(1, SIDE * SIDE)
-    def _(j):
-        tok_copy(j).wait_send()
-        res_copy(j).wait_send()
+    @pl.loop(0, CHUNKS)
+    def _(k):
+        for p in range(2):
+            others(k, p, lambda: tok_wait(k, p).wait_send())
+            others(k, p, lambda: res_copy(k, p).wait_send())
 
 
 def body(tokens, gate_weight, up_weight, down_weight, gate_mask, up_mask, down_mask):
@@ -337,17 +465,18 @@
             pltpu.VMEM((CHUNKS, 2, CORES, own_tokens, wide), F32),
             pltpu.VMEM((CHUNKS, 2, own_tokens, wide), F32),
             pltpu.VMEM((CHUNKS, 2, own_tokens, wide), BF16),
-            pltpu.VMEM((chips, own_tokens, wide), BF16),
+            pltpu.VMEM((CHUNKS, 2, own_tokens, wide), BF16),
+            pltpu.VMEM((own_tokens, wide), F32),
             dma((3, 4)),
             dma,
-            dma((chips,)), dma((chips,)),
+            dma((CHUNKS, 2)), dma((CHUNKS, 2)),
             dma((CHUNKS,)), dma((CHUNKS,)),
             dma((2, 3, CHUNKS)), dma((2, 3, CHUNKS)),
             dma((2, CHUNKS)), dma((2, CHUNKS)),
             dma((2, CHUNKS)), dma((2, CHUNKS)),
             dma((2, 4, CHUNKS)), dma((2, 4, CHUNKS)),
             dma((CHUNKS,)), dma((CHUNKS,)),
-            dma((chips,)), dma((chips,)),
+            dma((CHUNKS, 2)), dma((CHUNKS, 2)),
         ],
         compiler_params=pltpu.CompilerParams(
             collective_id=0, has_side_effects=True, vmem_limit_bytes=60 * 2**20

time: 132 us -> 112 us (0.85)
  Pallas kernels: 127 us -> 107 us
    pallas_call x1, Pallas kernels: 127 us -> 107 us  [body(): pl.pallas_call(kernel, out_shape=jax.ShapeDtypeStruct((own_tokens, wide),...]
where the time goes in v2:
time: 112 us; the launch traced here: 111 us
  Pallas kernels  107 us (96%)
  local copies, waits for them, and re-layouts  4.28 us (4%)
    pallas_call x1, Pallas kernels, body(): pl.pallas_call(kernel, out_shape=jax.ShapeDtypeStruct((own_tokens, wide),...  107 us
    unnamed x3, local copies, waits for them, and re-layouts  4.28 us

profile of v2, /device:TPU:2, one launch (start us, length us, event | category | flops | bytes accessed | tf_op | source)
XLA Modules:
  0.0 111.0 jit_solution(5131406860699993236)
XLA Ops:
  0.0 1.4 %copy.8.gate_mask = s32[16,7]{1,0:T(8,128)} copy(s32[16,7]{0,1:T(8,128)} %param.11) | data formatting | bytes 896 | tf_op args[4]
  1.4 1.4 %copy.9.up_mask = s32[16,7]{1,0:T(8,128)} copy(s32[16,7]{0,1:T(8,128)} %param.12) | data formatting | bytes 896 | tf_op args[5]
  2.7 106.7 %shard_map.73 = bf16[32,2048]{1,0:T(8,128)(2,1)} custom-call(s32[16,7]{1,0:T(8,128)} %copy.8.gate_mask, s32[16,7]{1,0:T(8,128)} %copy.9.up_mask, s32[7,16]{1,0:T(8,128)} %down_mask.1, bf16[32,2048]{1,0:T(8,128)(2,1)} %tokens.1, bf16[2048,896]{1,0:T(8,128)(2,1)} %gate_weight.1, bf16[2048,896]{1,0:T(8,128)(2,1)} %up_weight.1, bf16[896,2048]{1,0:T(8,128)(2,1)} %down_weight.1), custom_call_target="tpu_custom_call" | custom-call | flops 11274289152 | bytes 11010048 | tf_op jit(solution)/shard_map/pallas_call | solution.py:448
  109.4 1.6 %copy.11 = bf16[32,2048]{1,0:T(8,128)(2,1)} copy(bf16[32,2048]{1,0:T(8,128)(2,1)} %shard_map.73) | data formatting | bytes 262144

commit v3 on v2

--- a/solution.py
+++ b/solution.py
@@ -64,11 +64,11 @@
     "gather_end",
     "sum_end",
     "sum3",
+    "send_result",
     "sum2",
     "sum1",
     "bring_late",
     "matmul",
-    "send_result",
     "collect",
 )
 DX, DY = (
@@ -206,16 +206,23 @@
         device = second[side] if s == 3 else neighbour[side]
         return remote(block, block, ag_send.at[side, s, c], ag_recv.at[side, s, c], device)
 
-    def ex_copy(c):
+    parts = tuple(slice(h * WIDTH2, (h + 1) * WIDTH2) for h in range(down.shape[1] // WIDTH2))
+
+    def ex_copy(c, h):
         return remote(
-            term.at[c, :, 1 - core], sibling.at[c], ex_send.at[c], ex_recv.at[c], mate
+            term.at[c, :, 1 - core, :, parts[h]], sibling.at[c, :, :, parts[h]],
+            ex_send.at[c, h], ex_recv.at[c, h], mate,
         )
 
-    def res_copy(k, p):
+    def res_copy(k, p, h):
         return remote(
-            out_send.at[k, p], out_recv.at[k, p], res_send.at[k, p], res_recv.at[k, p],
-            at_offset(k, p, 1, core),
+            out_send.at[k, p, :, parts[h]], out_recv.at[k, p, :, parts[h]],
+            res_send.at[k, p, h], res_recv.at[k, p, h], at_offset(k, p, 1, core),
         )
+
+    def each_part(run):
+        for h in range(len(parts)):
+            run(h)
 
     def keep(ref, rows, lanes, flag):
         scale = jnp.full((BLOCK, BLOCK), flag.astype(F32), F32).astype(BF16)
@@ -248,13 +255,12 @@
             part[pl.ds(c, GROUP), :, :, lanes] = value.reshape(GROUP, ROWS, OWN, WIDTH1)
 
     def down_matmul(c):
-        @pl.loop(0, down.shape[1] // WIDTH2)
-        def _(n):
-            lanes = pl.ds(pl.multiple_of(n * WIDTH2, WIDTH2), WIDTH2)
+        for h, lanes in enumerate(parts):
             value = jnp.dot(
                 hid[c].reshape(ROWS * OWN, ff), down[:, lanes], preferred_element_type=F32
             )
             term[c, :, :, :, lanes] = value.reshape(2, CORES, 2 * OWN, WIDTH2)
+            ex_copy(c, h).start()
 
     def sum_start(c):
         owner = ring(4)
@@ -306,15 +312,15 @@
             ag_copy(side, 2, c).wait_recv()
             ag_copy(side, 3, c).wait_recv()
         down_matmul(c)
-        ex_copy(c).start()
 
     def send_result(c):
-        ex_copy(c).wait_recv()
-        for p in range(2):
-            value = term[c, p, core] + sibling[c, p]
-            term[c, p, core] = value
-            out_send[c, p] = value.astype(BF16)
-            others(c, p, lambda: res_copy(c, p).start())
+        for h, lanes in enumerate(parts):
+            ex_copy(c, h).wait_recv()
+            for p in range(2):
+                value = term[c, p, core, :, lanes] + sibling[c, p, :, lanes]
+                term[c, p, core, :, lanes] = value
+                out_send[c, p, :, lanes] = value.astype(BF16)
+                others(c, p, lambda: res_copy(c, p, h).start())
 
     send_wave(0)
     for i in range(4):
@@ -378,7 +384,7 @@
 
     def collect(c):
         for p in range(2):
-            others(c, p, lambda: res_copy(c, p).wait_recv())
+            others(c, p, lambda: each_part(lambda h: res_copy(c, p, h).wait_recv()))
 
         @pl.when(c == 0)
         def _():
@@ -410,12 +416,12 @@
             stages[name](t)
 
     late = ((6, 0), (6, 1), (7, 0), (7, 1))
-    for place in late:
-        res_copy(*place).wait_recv()
-    total = acc[...]
-    for k, p in late:
-        total = total + out_recv[k, p].astype(F32)
-    out[...] = total.astype(BF16)
+    for h, lanes in enumerate(parts):
+        total = acc[:, lanes]
+        for k, p in late:
+            res_copy(k, p, h).wait_recv()
+            total = total + out_recv[k, p, :, lanes].astype(F32)
+        out[:, lanes] = total.astype(BF16)
 
     @pl.loop(0, CHUNKS)
     def _(c):
@@ -427,13 +433,13 @@
             for s in range(4):
                 ag_copy(side, s, c).wait_send()
         fwd_copy(c).wait_send()
-        ex_copy(c).wait_send()
+        each_part(lambda h: ex_copy(c, h).wait_send())
 
     @pl.loop(0, CHUNKS)
     def _(k):
         for p in range(2):
             others(k, p, lambda: tok_wait(k, p).wait_send())
-            others(k, p, lambda: res_copy(k, p).wait_send())
+            others(k, p, lambda: each_part(lambda h: res_copy(k, p, h).wait_send()))
 
 
 def body(tokens, gate_weight, up_weight, down_weight, gate_mask, up_mask, down_mask):
@@ -475,8 +481,8 @@
             dma((2, CHUNKS)), dma((2, CHUNKS)),
             dma((2, CHUNKS)), dma((2, CHUNKS)),
             dma((2, 4, CHUNKS)), dma((2, 4, CHUNKS)),
-            dma((CHUNKS,)), dma((CHUNKS,)),
             dma((CHUNKS, 2)), dma((CHUNKS, 2)),
+            dma((CHUNKS, 2, 2)), dma((CHUNKS, 2, 2)),
         ],
         compiler_params=pltpu.CompilerParams(
             collective_id=0, has_side_effects=True, vmem_limit_bytes=60 * 2**20

time: 112 us -> 112 us (level)
  no operation moved by 1% of the time
where the time goes in v3:
time: 112 us; the launch traced here: 111 us
  Pallas kernels  107 us (96%)
  local copies, waits for them, and re-layouts  4.28 us (4%)
    pallas_call x1, Pallas kernels, body(): pl.pallas_call(kernel, out_shape=jax.ShapeDtypeStruct((own_tokens, wide),...  107 us
    unnamed x3, local copies, waits for them, and re-layouts  4.28 us

profile of v3, /device:TPU:2, one launch (start us, length us, event | category | flops | bytes accessed | tf_op | source)
XLA Modules:
  0.0 111.3 jit_solution(9905526444453567072)
XLA Ops:
  0.0 1.4 %copy.8.gate_mask = s32[16,7]{1,0:T(8,128)} copy(s32[16,7]{0,1:T(8,128)} %param.11) | data formatting | bytes 896 | tf_op args[4]
  1.4 1.4 %copy.9.up_mask = s32[16,7]{1,0:T(8,128)} copy(s32[16,7]{0,1:T(8,128)} %param.12) | data formatting | bytes 896 | tf_op args[5]
  2.7 107.0 %shard_map.73 = bf16[32,2048]{1,0:T(8,128)(2,1)} custom-call(s32[16,7]{1,0:T(8,128)} %copy.8.gate_mask, s32[16,7]{1,0:T(8,128)} %copy.9.up_mask, s32[7,16]{1,0:T(8,128)} %down_mask.1, bf16[32,2048]{1,0:T(8,128)(2,1)} %tokens.1, bf16[2048,896]{1,0:T(8,128)(2,1)} %gate_weight.1, bf16[2048,896]{1,0:T(8,128)(2,1)} %up_weight.1, bf16[896,2048]{1,0:T(8,128)(2,1)} %down_weight.1), custom_call_target="tpu_custom_call" | custom-call | flops 11274289152 | bytes 11010048 | tf_op jit(solution)/shard_map/pallas_call | solution.py:454
  109.7 1.6 %copy.11 = bf16[32,2048]{1,0:T(8,128)(2,1)} copy(bf16[32,2048]{1,0:T(8,128)(2,1)} %shard_map.73) | data formatting | bytes 262144
